TPU v7x, 256 devices: a whole 4x4x8 slice. The times are simulated.
256 devices in a mesh: blk: 32 (over y, z), section: 4 (over x_hi, core), batch: 2 (over x_lo).
Axes of the slice: x: 4 (x_hi: 2, x_lo: 2; x = x_hi * 2 + x_lo), y: 4, z: 8, core: 2. Of those that a mesh axis runs over, the one named last changes fastest.
Arguments:
- latent: bfloat16 [16384, 3072], P(('batch', 'blk')), parts along dimension 0, may hold values from -48 to 48
- stale_kv: bfloat16 [2, 16384, 1536], P(None, ('batch', 'blk'), 'section'), parts along dimension 1, may hold values from -64 to 64
- text_kv: bfloat16 [2, 1024, 1536], P(None, 'batch', 'section'), parts along dimension 1, may hold values from -9 to 9
- text_count: int32 [2], P('batch'), parts along dimension 0, may hold values from 128 to 512
- timestep: int32 [2], P('batch'), parts along dimension 0, may hold values from 0 to 27
- modulation: bfloat16 [28, 9216], replicated, may hold values from -4 to 4
- w_qkv: bfloat16 [3072, 3, 1536], P(None, None, 'section'), may hold values from -0.109375 to 0.109375
- w_out: bfloat16 [1536, 3072], P('section'), may hold values from -0.15625 to 0.15625
- norm_gain: float32 [2, 128], replicated, may hold values from 1.2 to 2.6
Outputs:
- layer_out: bfloat16 [16384, 3072], P(('batch', 'blk'), 'section'), parts along dimension 0
- next_cache: bfloat16 [2, 16384, 1536], P(None, ('batch', 'blk'), 'section'), parts along dimension 1
There are 2 independent parts, one for each index of `batch`. A program takes and returns all parts, laid end to end along the dimension named above; an argument that names none is the same for every part. Nothing has to cross between parts.
All inputs are finite; a program needn't handle non-finite values.
Results may differ from a plain program's by a relative error of at most 0.0075.
Values may be sent and summed in bfloat16 or wider, within the bound.
A program may use at most 128 MiB of HBM per device.

v0:
```python
import math

import jax
import jax.numpy as jnp
from jax import lax
from jax.sharding import PartitionSpec as P

HD = 128


def head_norm(block, gain):
    square_mean = jnp.mean(block * block, axis=-1, keepdims=True)
    return (block * lax.rsqrt(square_mean + 1e-06) * gain).astype(jnp.bfloat16)


def local(latent, stale_kv, text_kv, text_count, timestep, modulation, w_qkv, w_out, norm_gain):
    row_count = latent.shape[0]
    width = latent.shape[1]
    local_inner = w_qkv.shape[2]
    heads_here = local_inner // HD
    patch_index = lax.axis_index("blk")
    own_start = patch_index * row_count
    mod_row = lax.dynamic_slice_in_dim(modulation, timestep[0], 1, 0)[0].astype(jnp.float32)
    shift_part = mod_row[:width]
    scale_part = mod_row[width : 2 * width]
    gate_part = mod_row[2 * width :]
    hidden_float = latent.astype(jnp.float32)
    row_mean = jnp.mean(hidden_float, axis=1, keepdims=True)
    centered = hidden_float - row_mean
    row_var = jnp.mean(centered * centered, axis=1, keepdims=True)
    normed = (centered * lax.rsqrt(row_var + 1e-06) * (1.0 + scale_part) + shift_part).astype(
        jnp.bfloat16
    )
    projected = jnp.dot(
        normed, w_qkv.reshape(width, 3 * local_inner), preferred_element_type=jnp.float32
    )
    query_part = head_norm(
        projected[:, :local_inner].reshape(row_count, heads_here, HD), norm_gain[0]
    )
    key_part = head_norm(
        projected[:, local_inner : 2 * local_inner].reshape(row_count, heads_here, HD), norm_gain[1]
    )
    value_part = projected[:, 2 * local_inner :].astype(jnp.bfloat16)
    fresh_pairs = jnp.stack([key_part.reshape(row_count, local_inner), value_part])
    cache_all = lax.all_gather(stale_kv, "blk", axis=1, tiled=True)
    image_pairs = lax.dynamic_update_slice_in_dim(cache_all, fresh_pairs, own_start, 1)
    all_pairs = jnp.concatenate([text_kv, image_pairs], axis=1)
    total_keys = all_pairs.shape[1]
    key_all = all_pairs[0].reshape(total_keys, heads_here, HD)
    value_all = all_pairs[1].reshape(total_keys, heads_here, HD)
    text_valid = jnp.arange(text_kv.shape[1]) < text_count[0]
    valid = jnp.concatenate([text_valid, jnp.ones((image_pairs.shape[1],), bool)])
    scores = jnp.einsum("qhd,khd->hqk", query_part, key_all, preferred_element_type=jnp.float32) * (
        1.0 / math.sqrt(HD)
    )
    scores = jnp.where(valid[None, None, :], scores, -jnp.inf)
    top_score = jnp.max(scores, axis=2, keepdims=True)
    expo = jnp.exp(scores - top_score)
    probs = (expo / jnp.sum(expo, axis=2, keepdims=True)).astype(jnp.bfloat16)
    attended = jnp.einsum("hqk,khd->qhd", probs, value_all, preferred_element_type=jnp.float32)
    attended = attended.astype(jnp.bfloat16).reshape(row_count, local_inner)
    partial_branch = jnp.dot(attended, w_out, preferred_element_type=jnp.float32)
    summed = lax.psum_scatter(
        partial_branch.astype(jnp.bfloat16), "section", scatter_dimension=1, tiled=True
    ).astype(jnp.float32)
    column_count = summed.shape[1]
    column_start = lax.axis_index("section") * column_count
    hidden_piece = lax.dynamic_slice_in_dim(hidden_float, column_start, column_count, 1)
    gate_piece = lax.dynamic_slice_in_dim(gate_part, column_start, column_count, 0)
    layer_out = (hidden_piece + gate_piece * summed).astype(jnp.bfloat16)
    return (layer_out, fresh_pairs)


def solution(mesh):
    in_specs = (
        P(("batch", "blk"), None),
        P(None, ("batch", "blk"), "section"),
        P(None, "batch", "section"),
        P("batch"),
        P("batch"),
        P(),
        P(None, None, "section"),
        P("section", None),
        P(),
    )
    out_specs = (P(("batch", "blk"), "section"), P(None, ("batch", "blk"), "section"))
    return jax.shard_map(local, mesh=mesh, in_specs=in_specs, out_specs=out_specs, check_vma=False)
```

profile of v0, /device:TPU:1, one launch (start us, length us, event | category | flops | bytes accessed | tf_op | source)
XLA Modules:
  0.0 237.6 jit_solution(13653135179792501405)
XLA Ops:
  7.2 2.1 copy.14
  9.4 10.3 %copy.15 = bf16[3072,3,384]{0,2,1:T(8,128)(2,1)} copy(bf16[3072,3,384]{2,0,1:T(8,128)(2,1)} %param.15) | data formatting | bytes 14155776 | tf_op args[6]
  20.3 1.7 convert_reduce_fusion
  22.0 2.0 multiply_reduce_fusion
  24.0 0.9 dynamic-slice_convert_fusion
  25.6 6.3 %fusion.4 = f32[256,1152]{1,0:T(8,128)S(1)} fusion(bf16[3072,1152]{0,1:T(8,128)(2,1)} %bitcast.33, bf16[256,3072]{1,0:T(8,128)(2,1)} %param.9, f32[3072]{0:T(1024)S(1)} %bitcast.40, f32[3072]{0:T(1024)S(1)} %bitcast.41, f32[256]{0:T(256)S(1)} %add_rsqrt_fusion.2, f32[256]{0:T(256)S(1)} %broadcast_multiply_fusion), kind=kOutput, calls=%fused_computation.14 | convolution fusion | flops 1816657920 | bytes 9857024 | tf_op jit(solution)/shard_map/dot_general | solution.py:34
  32.6 1.9 copy.16
  34.6 1.0 reduce_sum.47
  35.6 0.8 mul.103
  36.4 1.9 copy.17
  38.9 1.8 fusion.17
  40.8 1.0 copy.18
  41.8 1.4 copy.19
  43.9 1.2 copy.20
  45.1 94.5 %all-gather.2.cloned.1.call-done = bf16[2,8192,384]{1,2,0:T(8,128)(2,1)} async-done(((bf16[2,256,384]{1,2,0:T(8,128)(2,1)}), bf16[2,8192,384]{1,2,0:T(8,128)(2,1)}) %all-gather.2.cloned.1.call-update) | async-done | bytes 12582928 | tf_op jit(solution)/shard_map/all_gather | solution.py:45
  139.6 1.9 constant_dynamic-update-slice_fusion
  141.5 7.5 %pad_maximum_fusion = (bf16[1,8704,384]{1,2,0:T(8,128)(2,1)S(1)}, bf16[1,8704,384]{1,2,0:T(8,128)(2,1)}) fusion(bf16[2,8192,384]{1,2,0:T(8,128)(2,1)} %constant_dynamic-update-slice_fusion, bf16[2,512,384]{1,2,0:T(8,128)(2,1)S(1)} %copy.19), kind=kLoop, calls=%fused_computation.9 | loop fusion | flops 26738688 | bytes 26738688 | tf_op jit(solution)/shard_map/concatenate | solution.py:47
  149.0 11.0 %fusion = (f32[3,256]{1,0:T(4,128)S(1)}, f32[3,256,8704]{2,1,0:T(8,128)}) fusion(pred[8704]{0:T(1024)(128)(4,1)S(1)} %concatenate.7, bf16[8704,3,128]{0,2,1:T(8,128)(2,1)S(1)} %bitcast.32, f32[256,3,128]{0,2,1:T(8,128)S(1)} %bitcast.36, f32[128]{0:T(128)S(1)} %copy-done.2, f32[256,3]{0,1:T(4,128)S(1)} %add_rsqrt_fusion), kind=kOutput, calls=%fused_computation.3 | convolution fusion | flops 1731624192 | bytes 33831936 | tf_op jit(solution)/shard_map/qhd,khd->hqk/dot_general | solution.py:53
  160.1 12.1 %fusion.1 = f32[3,256]{1,0:T(4,128)S(1)} fusion(f32[3,256,8704]{2,1,0:T(8,128)} %get-tuple-element.12, f32[3,256]{1,0:T(4,128)S(1)} %get-tuple-element.11, pred[8704]{0:T(1024)(128)(4,1)S(1)} %concatenate.7), kind=kLoop, calls=%fused_computation.4 | loop fusion | flops 26737920 | bytes 26753536 | tf_op jit(solution)/shard_map/reduce_sum | solution.py:59
  172.1 14.8 %fusion.9 = bf16[3,128,256]{2,1,0:T(8,128)(2,1)S(1)} fusion(bf16[8704,3,128]{0,2,1:T(8,128)(2,1)} %bitcast.34, f32[3,256,8704]{2,1,0:T(8,128)} %get-tuple-element.12, f32[3,256]{1,0:T(4,128)S(1)} %fusion.1, f32[3,256]{1,0:T(4,128)S(1)} %get-tuple-element.11, pred[8704]{0:T(1024)(128)(4,1)S(1)} %concatenate.7), kind=kOutput, calls=%fused_computation.19 | convolution fusion | flops 1744797696 | bytes 33634816 | tf_op jit(solution)/shard_map/hqk,khd->qhd/dot_general | solution.py:60
  187.0 2.1 convolution_convert_fusion
  189.1 3.4 %convert_element_type.39 = f32[256,3072]{1,0:T(8,128)} convert(bf16[256,3072]{1,0:T(8,128)(2,1)} %param.9) | non-fusion elementwise | flops 786432 | bytes 4718592 | tf_op jit(solution)/shard_map/convert_element_type | solution.py:27
  193.3 35.4 %reduce-scatter.2.cloned.1.call-done = bf16[256,768]{1,0:T(8,128)(2,1)} async-done(((bf16[256,3072]{1,0:T(8,128)(2,1)}), bf16[256,768]{1,0:T(8,128)(2,1)}) %reduce-scatter.2.cloned.1.call-update) | async-done | bytes 393232 | tf_op jit(solution)/shard_map/reduce_scatter | solution.py:63
  228.7 2.1 add_convert_fusion.2
  (26 shorter events, 2.9 us)
Async XLA Ops:
  7.2 179.8 %copy-start = (bf16[384,3072]{1,0:T(8,128)(2,1)S(1)}, bf16[384,3072]{1,0:T(8,128)(2,1)}, u32[]{:S(2)}) copy-start(bf16[384,3072]{1,0:T(8,128)(2,1)} %param.16) | copy-start | bytes 7077892
  7.2 132.4 %all-gather.2.cloned.1.call-start = ((), (), s32[]{:S(2)}) async-start(), calls=%async_computation.1 | async-start | bytes 12976128 | tf_op jit(solution)/shard_map/all_gather | solution.py:45
  9.3 219.4 %reduce-scatter.2.cloned.1.call-start = ((), (), s32[]{:S(2)}) async-start(), calls=%async_computation.2 | async-start | bytes 1966080 | tf_op jit(solution)/shard_map/reduce_scatter | solution.py:63
  25.6 12.8 %copy-start.3 = (f32[2,128]{1,0:T(2,128)S(1)}, f32[2,128]{1,0:T(2,128)}, u32[]{:S(2)}) copy-start(f32[2,128]{1,0:T(2,128)} %param.17) | copy-start | bytes 3076
  40.8 3.0 %copy-start.1 = (bf16[2,256,384]{2,1,0:T(8,128)(2,1)}, bf16[2,256,384]{2,1,0:T(8,128)(2,1)S(1)}, u32[]{:S(2)}) copy-start(bf16[2,256,384]{2,1,0:T(8,128)(2,1)S(1)} %pad_maximum_fusion.1) | copy-start | bytes 1179652
  141.5 7.6 %copy-start.2 = (f32[128]{0:T(128)S(1)}, f32[128]{0:T(128)}, u32[]{:S(2)}) copy-start(f32[128]{0:T(128)} %get-tuple-element.9) | copy-start | bytes 1540
Sparse Core Ops, SparseCore 0:
  11.1 128.5 all-gather.1
  189.3 39.3 reduce-scatter.1
where the time goes:
time: 239 us; the launch traced here: 238 us
  waiting for transfers between devices  130 us (54%)
  matrix products  34.3 us (14%)
  other arithmetic  34.2 us (14%)
  local copies, waits for them, and re-layouts  23.7 us (10%)
  between operations  15.5 us (6%)
    all_gather x1, waiting for transfers between devices, local(): cache_all = lax.all_gather(stale_kv, 'blk', axis=1, tiled=True)  94.5 us
    reduce_scatter x1, waiting for transfers between devices, local(): lax.psum_scatter(partial_branch.astype(jnp.bfloat16), 'section', scatter_...  35.4 us
    dot_general x1, matrix products, local(): jnp.einsum('hqk,khd->qhd', probs, value_all, preferred_element_type=jnp.f...  14.8 us
    unnamed x11, local copies, waits for them, and re-layouts  13.8 us
    reduce_sum x1, other arithmetic, local(): probs = (expo / jnp.sum(expo, axis=2, keepdims=True)).astype(jnp.bfloat16)  12.1 us
    dot_general x1, matrix products, local(): jnp.einsum('qhd,khd->hqk', query_part, key_all, preferred_element_type=jn...  11 us
    concatenate x1, other arithmetic, local(): all_pairs = jnp.concatenate([text_kv, image_pairs], axis=1)  7.55 us
    dot_general x1, matrix products, local(): jnp.dot(normed, w_qkv.reshape(width, 3 * local_inner), preferred_element_...  6.28 us
  transfers between devices with their start and end apart: 2, of which 2 were waited for; matrix products, arithmetic and copies ran while one was open for 16% of the time, Pallas kernels for 0%

commit v1 on v0

v1 whole, which is shorter than its diff:
```python
import functools
import math

import jax
import jax.numpy as jnp
from jax import lax
from jax.experimental import pallas as pl
from jax.experimental.pallas import tpu as pltpu
from jax.sharding import PartitionSpec as P

MESH = pl.DeviceIdType.MESH
HD = 128
NY, NZ = 4, 8
HALF = NZ // 2
HEADS = 3
SECTIONS = 4
TOK = 256
TXT = 512
WIDTH = 3072
COLS = WIDTH // SECTIONS
PIECES = 2
ROWS = TOK // PIECES
SCORE_SCALE = math.log2(math.e) / math.sqrt(HD)


def kernel(
    text_count, timestep, modulation, gain, latent, stale, text, w_qkv, w_out,
    layer_out, next_cache,
    lat_v, normed, w_v, text_v, kv, fresh, q_all, acc, top, den,
    o_send, o_recv, s_send, s_recv, att, w_all, branch,
    kv_ss, kv_rs, q_ss, q_rs, w_ss, w_rs, o_ss, o_rs, s_ss, s_rs, a_ss, a_rs,
    lat_sem, wq_sem, text_sem, own_sem, cache_sem, wo_sem,
):
    blk = lax.axis_index("blk")
    sec = lax.axis_index("section")
    y, z = blk // NZ, blk % NZ

    def at_y(k):
        return {"blk": ((y + k + NY) % NY) * NZ + z}

    def at_sec(j):
        return {"section": (sec + j) % SECTIONS}

    right = {"blk": y * NZ + (z + 1) % NZ}
    left = {"blk": y * NZ + (z + NZ - 1) % NZ}
    friends = [right, left] + [at_y(k) for k in range(1, NY)] + [at_sec(j) for j in range(1, SECTIONS)]
    barrier = pltpu.get_barrier_semaphore()
    for friend in friends:
        pl.semaphore_signal(barrier, inc=1, device_id=friend, device_id_type=MESH)

    def head_cols(h):
        return pl.ds(h * HD, HD)

    lat_copy = pltpu.make_async_copy(latent, lat_v, lat_sem)
    lat_copy.start()
    wq_copies = [pltpu.make_async_copy(w_qkv.at[c], w_v.at[c], wq_sem.at[c]) for c in range(3)]
    for copy in wq_copies:
        copy.start()
    text_copies = [
        pltpu.make_async_copy(text.at[:, :, head_cols(h)], text_v.at[h], text_sem.at[h]) for h in range(HEADS)
    ]
    own_copies = [
        pltpu.make_async_copy(stale.at[:, :, head_cols(h)], kv.at[0, h], own_sem.at[h]) for h in range(HEADS)
    ]
    wo_copy = pltpu.make_async_copy(
        w_out.at[:, :, pl.ds(pl.multiple_of(sec * COLS, COLS), COLS)], w_all.at[:, sec], wo_sem
    )
    for copy in text_copies + own_copies + [wo_copy]:
        copy.start()

    pl.semaphore_wait(barrier, len(friends))

    def ring(h, d, side, piece):
        rows = pl.ds(piece * ROWS, ROWS)
        into = d if side == 0 else NZ - d
        source = stale.at[:, rows, head_cols(h)] if d == 1 else kv.at[d - 1 if side == 0 else NZ - d + 1, h, :, rows, :]
        return pltpu.make_async_remote_copy(
            src_ref=source,
            dst_ref=kv.at[into, h, :, rows, :],
            send_sem=kv_ss.at[side, d, h, piece],
            recv_sem=kv_rs.at[side, d, h, piece],
            device_id=right if side == 0 else left,
            device_id_type=MESH,
        )

    def parts(d):
        return [
            (side, piece) for piece in range(PIECES) for side in range(2)
            if d < HALF or (piece < PIECES // 2) == (side == 0)
        ]

    def arrive(h, d):
        onward = parts(d + 1) if d < HALF else []
        for side, piece in parts(d):
            ring(h, d, side, piece).wait_recv()
            if (side, piece) in onward:
                ring(h, d + 1, side, piece).start()

    for h in range(HEADS):
        for side, piece in parts(1):
            ring(h, 1, side, piece).start()

    def w_send(j):
        to = lax.rem(sec + j, SECTIONS)
        return pltpu.make_async_remote_copy(
            src_ref=w_out.at[:, :, pl.ds(pl.multiple_of(to * COLS, COLS), COLS)],
            dst_ref=w_all.at[:, sec],
            send_sem=w_ss.at[j],
            recv_sem=w_rs.at[j],
            device_id=at_sec(j),
            device_id_type=MESH,
        )

    for j in range(1, SECTIONS):
        w_send(j).start()

    steps = lax.broadcasted_iota(jnp.int32, modulation.shape, 0)
    mod_row = jnp.sum(
        jnp.where(steps == timestep[0], modulation[...].astype(jnp.float32), 0.0), axis=0, keepdims=True
    )
    shift, scale, gate = (mod_row[:, i * WIDTH : (i + 1) * WIDTH] for i in range(3))
    scale = 1.0 + scale
    lat_copy.wait()

    chunk = 16

    def norm_rows(i, _):
        rows = pl.ds(pl.multiple_of(i * chunk, chunk), chunk)
        x = lat_v[rows, :].astype(jnp.float32)
        centered = x - jnp.mean(x, axis=1, keepdims=True)
        var = jnp.mean(centered * centered, axis=1, keepdims=True)
        normed[rows, :] = (centered * lax.rsqrt(var + 1e-06) * scale + shift).astype(jnp.bfloat16)
        return 0

    lax.fori_loop(0, TOK // chunk, norm_rows, 0)

    def project(c):
        wq_copies[c].wait()
        return jnp.dot(normed[...], w_v[c], preferred_element_type=jnp.float32)

    def head_norm(block, g):
        square = jnp.mean(block * block, axis=-1, keepdims=True)
        return (block * lax.rsqrt(square + 1e-06) * g).astype(jnp.bfloat16)

    def q_send(h, k):
        return pltpu.make_async_remote_copy(
            src_ref=q_all.at[h, 0],
            dst_ref=q_all.at[h, k],
            send_sem=q_ss.at[h, k],
            recv_sem=q_rs.at[h, k],
            device_id=at_y(k),
            device_id_type=MESH,
        )

    projected = project(0)
    for h in range(HEADS):
        q_all[h, 0] = head_norm(projected[:, h * HD : (h + 1) * HD], gain[0:1, :])
        for k in range(1, NY):
            q_send(h, k).start()
    arrive(0, 1)
    projected = project(1)
    for h in range(HEADS):
        fresh[h, 0] = head_norm(projected[:, h * HD : (h + 1) * HD], gain[1:2, :])
    arrive(1, 1)
    projected = project(2)
    for h in range(HEADS):
        fresh[h, 1] = projected[:, h * HD : (h + 1) * HD].astype(jnp.bfloat16)
    arrive(2, 1)
    cache_copies = [
        pltpu.make_async_copy(fresh.at[h], next_cache.at[:, :, head_cols(h)], cache_sem.at[h]) for h in range(HEADS)
    ]
    for copy in cache_copies:
        copy.start()

    def scores(q, keys):
        s = lax.dot_general(q, keys, (((1,), (1,)), ((), ())), preferred_element_type=jnp.float32)
        return s * SCORE_SCALE

    def attend(h, k, blocks, first):
        q = q_all[h, k]
        logits = []
        for keys, _, live in blocks:
            s = scores(q, keys)
            if live is not None:
                s = jnp.where(live, s, -jnp.inf)
            logits.append(s)
        best = functools.reduce(jnp.maximum, [jnp.max(s, axis=1, keepdims=True) for s in logits])
        if not first:
            before = top[h, k][:, 0:1]
            best = jnp.maximum(before, best)
        total = None
        for s, (_, values, _) in zip(logits, blocks):
            p = jnp.exp2(s - best).astype(jnp.bfloat16)
            ones = jnp.ones(values.shape, jnp.bfloat16)
            part = jnp.dot(p, jnp.concatenate([values, ones], axis=1), preferred_element_type=jnp.float32)
            total = part if total is None else total + part
        new_acc, new_den = total[:, :HD], total[:, HD:]
        if not first:
            fade = jnp.exp2(before - best)
            new_acc = new_acc + acc[h, k] * fade
            new_den = new_den + den[h, k] * fade
        acc[h, k] = new_acc
        den[h, k] = new_den
        top[h, k] = jnp.broadcast_to(best, (TOK, HD))

    def own_step(h):
        live = lax.broadcasted_iota(jnp.int32, (TOK, TXT), 1) < text_count[0]
        attend(h, 0, [(fresh[h, 0], fresh[h, 1], None), (text_v[h, 0], text_v[h, 1], live)], True)

        def one(k, _):
            attend(h, k, [(kv[0, h, 0], kv[0, h, 1], None)], True)
            return 0

        lax.fori_loop(1, NY, one, 0)

    def pair_step(h, d):
        def one(k, _):
            attend(h, k, [(kv[i, h, 0], kv[i, h, 1], None) for i in (d, NZ - d)], False)
            return 0

        lax.fori_loop(0, NY, one, 0)

    for copy in text_copies + own_copies:
        copy.wait()
    for h in range(HEADS):
        for k in range(1, NY):
            q_send(h, k).wait_recv()

    for d in range(2, HALF):
        def ring_step(h, _, d=d):
            arrive(h, d)
            if d == 2:
                own_step(h)
            pair_step(h, d - 1)
            return 0

        lax.fori_loop(0, HEADS, ring_step, 0)

    def last_pairs(h, _):
        pair_step(h, HALF - 1)
        return 0

    lax.fori_loop(0, HEADS, last_pairs, 0)

    def o_copies(h, k):
        return [
            pltpu.make_async_remote_copy(
                src_ref=a.at[h, k],
                dst_ref=b.at[h, k],
                send_sem=ss.at[h, k],
                recv_sem=rs.at[h, k],
                device_id=at_y(-k),
                device_id_type=MESH,
            )
            for a, b, ss, rs in ((o_send, o_recv, o_ss, o_rs), (s_send, s_recv, s_ss, s_rs))
        ]

    def opposite(h, k):
        attend(h, k, [(kv[HALF, h, 0], kv[HALF, h, 1], None)], False)

    def finish(h):
        arrive(h, HALF)

        def one(k, _):
            opposite(h, k)
            total = den[h, k]
            o_send[h, k] = (acc[h, k] / total).astype(jnp.bfloat16)
            lse = top[h, k] + jnp.log2(total)
            for i in range(TOK // HD):
                s_send[h, k, :, i * HD : (i + 1) * HD] = lse[i * HD : (i + 1) * HD, :].T[0:8, :]
            for copy in o_copies(h, k):
                copy.start()
            return 0

        lax.fori_loop(1, NY, one, 0)
        opposite(h, 0)

    def a_send(h, j):
        return pltpu.make_async_remote_copy(
            src_ref=att.at[h, sec],
            dst_ref=att.at[h, sec],
            send_sem=a_ss.at[h, j],
            recv_sem=a_rs.at[h, j],
            device_id=at_sec(j),
            device_id_type=MESH,
        )

    def merge(h):
        total = den[h, 0]
        outs = [acc[h, 0] / total]
        lses = [top[h, 0] + jnp.log2(total)]
        for k in range(1, NY):
            for copy in o_copies(h, k):
                copy.wait_recv()
            outs.append(o_recv[h, k].astype(jnp.float32))
            stat = s_recv[h, k]
            lses.append(
                jnp.concatenate(
                    [
                        jnp.broadcast_to(stat[0:1, i * HD : (i + 1) * HD], (HD, HD)).T
                        for i in range(TOK // HD)
                    ],
                    axis=0,
                )
            )
        best = functools.reduce(jnp.maximum, lses)
        weights = [jnp.exp2(lse - best) for lse in lses]
        blend = functools.reduce(jnp.add, [o * w for o, w in zip(outs, weights)])
        att[h, sec] = (blend / functools.reduce(jnp.add, weights)).astype(jnp.bfloat16)
        for j in range(1, SECTIONS):
            a_send(h, j).start()

    def out_project(h):
        for j in range(1, SECTIONS):
            a_send(h, j).wait_recv()
        heads = jnp.concatenate([att[h, s] for s in range(SECTIONS)], axis=1)
        return jnp.dot(heads, w_all[h].reshape(SECTIONS * HD, COLS), preferred_element_type=jnp.float32)

    finish(0)
    finish(1)
    merge(0)
    finish(2)
    merge(1)
    wo_copy.wait()
    for j in range(1, SECTIONS):
        w_send(j).wait_recv()
    branch[...] = out_project(0)
    merge(2)
    branch[...] += out_project(1)
    columns = pl.ds(pl.multiple_of(sec * COLS, COLS), COLS)
    steps = lax.broadcasted_iota(jnp.int32, (modulation.shape[0], COLS), 0)
    gate_cols = modulation[:, pl.ds(pl.multiple_of(2 * WIDTH + sec * COLS, COLS), COLS)].astype(jnp.float32)
    gate_row = jnp.sum(jnp.where(steps == timestep[0], gate_cols, 0.0), axis=0, keepdims=True)
    summed = branch[...] + out_project(2)
    layer_out[...] = (lat_v[:, columns].astype(jnp.float32) + gate_row * summed).astype(jnp.bfloat16)

    for h in range(HEADS):
        for d in range(1, HALF + 1):
            for side, piece in parts(d):
                ring(h, d, side, piece).wait_send()
        for k in range(1, NY):
            q_send(h, k).wait_send()
            for copy in o_copies(h, k):
                copy.wait_send()
        for j in range(1, SECTIONS):
            a_send(h, j).wait_send()
    for j in range(1, SECTIONS):
        w_send(j).wait_send()
    for copy in cache_copies:
        copy.wait()


def local(latent, stale_kv, text_kv, text_count, timestep, modulation, w_qkv, w_out, norm_gain):
    vmem = pl.BlockSpec(memory_space=pltpu.VMEM)
    smem = pl.BlockSpec(memory_space=pltpu.SMEM)
    hbm = pl.BlockSpec(memory_space=pl.ANY)
    bf16, f32 = jnp.bfloat16, jnp.float32
    dma = pltpu.SemaphoreType.DMA
    return pl.pallas_call(
        kernel,
        out_shape=(
            jax.ShapeDtypeStruct((TOK, COLS), bf16),
            jax.ShapeDtypeStruct((2, TOK, HEADS * HD), bf16),
        ),
        in_specs=[smem, smem, vmem, vmem, hbm, hbm, hbm, hbm, hbm],
        out_specs=(vmem, hbm),
        scratch_shapes=[
            pltpu.VMEM((TOK, WIDTH), bf16),
            pltpu.VMEM((TOK, WIDTH), bf16),
            pltpu.VMEM((3, WIDTH, HEADS * HD), bf16),
            pltpu.VMEM((HEADS, 2, TXT, HD), bf16),
            pltpu.VMEM((NZ, HEADS, 2, TOK, HD), bf16),
            pltpu.VMEM((HEADS, 2, TOK, HD), bf16),
            pltpu.VMEM((HEADS, NY, TOK, HD), bf16),
            pltpu.VMEM((HEADS, NY, TOK, HD), f32),
            pltpu.VMEM((HEADS, NY, TOK, HD), f32),
            pltpu.VMEM((HEADS, NY, TOK, HD), f32),
            pltpu.VMEM((HEADS, NY, TOK, HD), bf16),
            pltpu.VMEM((HEADS, NY, TOK, HD), bf16),
            pltpu.VMEM((HEADS, NY, 8, TOK), f32),
            pltpu.VMEM((HEADS, NY, 8, TOK), f32),
            pltpu.VMEM((HEADS, SECTIONS, TOK, HD), bf16),
            pltpu.VMEM((HEADS, SECTIONS, HD, COLS), bf16),
            pltpu.VMEM((TOK, COLS), f32),
            dma((2, HALF + 1, HEADS, PIECES)), dma((2, HALF + 1, HEADS, PIECES)),
            dma((HEADS, NY)), dma((HEADS, NY)),
            dma((SECTIONS,)), dma((SECTIONS,)),
            dma((HEADS, NY)), dma((HEADS, NY)),
            dma((HEADS, NY)), dma((HEADS, NY)),
            dma((HEADS, SECTIONS)), dma((HEADS, SECTIONS)),
            dma, dma((3,)), dma((HEADS,)), dma((HEADS,)), dma((HEADS,)), dma,
        ],
        compiler_params=pltpu.CompilerParams(
            collective_id=1, has_side_effects=True, vmem_limit_bytes=52 << 20
        ),
    )(
        text_count, timestep, modulation, norm_gain, latent, stale_kv, text_kv,
        w_qkv.transpose(1, 0, 2), w_out.reshape(HEADS, HD, WIDTH),
    )


def solution(mesh):
    in_specs = (
        P(("batch", "blk"), None),
        P(None, ("batch", "blk"), "section"),
        P(None, "batch", "section"),
        P("batch"),
        P("batch"),
        P(),
        P(None, None, "section"),
        P("section", None),
        P(),
    )
    out_specs = (P(("batch", "blk"), "section"), P(None, ("batch", "blk"), "section"))
    return jax.shard_map(local, mesh=mesh, in_specs=in_specs, out_specs=out_specs, check_vma=False)
```

time: 239 us -> 84.8 us (0.35)
  waiting for transfers between devices: 130 us -> 0 us
  Pallas kernels: 0 us -> 78.4 us
  matrix products: 34.3 us -> 0 us
  other arithmetic: 34.2 us -> 0 us
  local copies, waits for them, and re-layouts: 23.7 us -> 4.22 us
  between operations: 15.5 us -> 1.94 us
    all_gather x1 -> x0, waiting for transfers between devices: 94.5 us -> none  [local(): cache_all = lax.all_gather(stale_kv, 'blk', axis=1, tiled=True)]
    pallas_call x0 -> x1, Pallas kernels: none -> 78.4 us  [local(): pl.pallas_call(kernel, out_shape=(jax.ShapeDtypeStruct((TOK, COLS), bf16)...]
    reduce_scatter x1 -> x0, waiting for transfers between devices: 35.4 us -> none  [local(): lax.psum_scatter(partial_branch.astype(jnp.bfloat16), 'section', scatter_...]
    dot_general x4 -> x0, matrix products: 34.3 us -> none  [the longest x1 14.8 us: local(): jnp.einsum('hqk,khd->qhd', probs, value_all, preferred_element_type=jnp.f...]
    reduce_sum x5 -> x0, other arithmetic: 16.8 us -> none  [the longest x1 12.1 us: local(): probs = (expo / jnp.sum(expo, axis=2, keepdims=True)).astype(jnp.bfloat16)]
    unnamed x11 -> x8, local copies, waits for them, and re-layouts: 13.8 us -> 4.22 us
    concatenate x1 -> x0, other arithmetic: 7.55 us -> none  [local(): all_pairs = jnp.concatenate([text_kv, image_pairs], axis=1)]
    convert_element_type x3 -> x0, other arithmetic: 6.48 us -> none  [the longest x1 3.44 us: local(): hidden_float = latent.astype(jnp.float32)]
  transfers between devices with their start and end apart: 2 -> 0, of which waited for: 2 -> 0; matrix products, arithmetic and copies ran while one was open for 16% -> 0% of each run, Pallas kernels for 0% -> 0%
where the time goes in v1:
time: 84.8 us; the launch traced here: 84.6 us
  Pallas kernels  78.4 us (92%)
  local copies, waits for them, and re-layouts  4.22 us (5%)
  between operations  1.94 us (2%)
    pallas_call x1, Pallas kernels, local(): pl.pallas_call(kernel, out_shape=(jax.ShapeDtypeStruct((TOK, COLS), bf16)...  78.4 us
    unnamed x8, local copies, waits for them, and re-layouts  4.22 us

profile of v1, /device:TPU:1, one launch (start us, length us, event | category | flops | bytes accessed | tf_op | source)
XLA Modules:
  0.0 84.6 jit_solution(15622950507728388050)
XLA Ops:
  1.9 0.0 copy-start
  1.9 1.1 %copy-done = bf16[28,9216]{1,0:T(8,128)(2,1)S(1)} copy-done((bf16[28,9216]{1,0:T(8,128)(2,1)S(1)}, bf16[28,9216]{1,0:T(8,128)(2,1)}, u32[]{:S(2)}) %copy-start) | copy-done | bytes 516120
  3.0 0.0 copy-start.1
  3.0 1.0 %copy-done.1 = bf16[2,256,384]{2,1,0:T(8,128)(2,1)S(1)} copy-done((bf16[2,256,384]{2,1,0:T(8,128)(2,1)S(1)}, bf16[2,256,384]{2,1,0:T(8,128)(2,1)}, u32[]{:S(2)}) %copy-start.1) | copy-done | bytes 393240
  4.0 0.0 copy-start.2
  4.0 0.7 copy-done.2
  4.7 78.4 %shard_map.104 = (bf16[256,768]{1,0:T(8,128)(2,1)S(1)}, bf16[2,256,384]{2,1,0:T(8,128)(2,1)S(1)}) custom-call(s32[1]{0:T(128)S(6)} %copy.13.text_count, s32[1]{0:T(128)S(6)} %copy.14.timestep, bf16[28,9216]{1,0:T(8,128)(2,1)S(1)} %copy-done, f32[2,128]{1,0:T(2,128)S(1)} %copy-done.2, bf16[256,3072]{1,0:T(8,128)(2,1)} %latent.1, ...), custom_call_target="tpu_custom_call" | custom-call | tf_op jit(solution)/shard_map/pallas_call | solution.py:359
  83.1 0.7 copy.15
  83.8 0.7 copy.16
Async XLA Ops:
  1.9 1.1 %copy-start = (bf16[28,9216]{1,0:T(8,128)(2,1)S(1)}, bf16[28,9216]{1,0:T(8,128)(2,1)}, u32[]{:S(2)}) copy-start(bf16[28,9216]{1,0:T(8,128)(2,1)} %modulation.1) | copy-start | bytes 1548292
  3.0 1.0 %copy-start.1 = (bf16[2,256,384]{2,1,0:T(8,128)(2,1)S(1)}, bf16[2,256,384]{2,1,0:T(8,128)(2,1)}, u32[]{:S(2)}) copy-start(bf16[2,256,384]{2,1,0:T(8,128)(2,1)} %stale.1) | copy-start | bytes 1179652
  4.0 0.7 copy-start.2

commit v2 on v1

v2 whole, which is shorter than its diff:
```python
import functools
import math

import jax
import jax.numpy as jnp
from jax import lax
from jax.experimental import pallas as pl
from jax.experimental.pallas import tpu as pltpu
from jax.sharding import PartitionSpec as P

MESH = pl.DeviceIdType.MESH
HD = 128
NY, NZ = 4, 8
HALF = NZ // 2
HEADS = 3
SECTIONS = 4
TOK = 256
TXT = 512
STEPS = 28
WIDTH = 3072
COLS = WIDTH // SECTIONS
PIECES = 2
ROWS = TOK // PIECES
PARTS = 2
PART = TOK // PARTS
EXTRA = 16
SCORE_SCALE = math.log2(math.e) / math.sqrt(HD)


def kernel(
    text_count, timestep, mod_in, gain_in, latent, stale, text, w_qkv, w_out,
    layer_out, next_cache,
    modulation, gain, lat_v, normed, w_v, text_v, kv, fresh, q_all, acc, top, den,
    o_send, o_recv, att, w_all, branch,
    kv_ss, kv_rs, q_ss, q_rs, w_ss, w_rs, o_ss, o_rs, a_ss, a_rs,
    mod_sem, gain_sem, lat_sem, wq_sem, text_sem, own_sem, cache_sem, wo_sem,
):
    blk = lax.axis_index("blk")
    sec = lax.axis_index("section")
    y, z = blk // NZ, blk % NZ

    def at_y(k):
        return {"blk": ((y + k + NY) % NY) * NZ + z}

    def at_sec(j):
        return {"section": (sec + j) % SECTIONS}

    right = {"blk": y * NZ + (z + 1) % NZ}
    left = {"blk": y * NZ + (z + NZ - 1) % NZ}
    friends = [right, left] + [at_y(k) for k in range(1, NY)] + [at_sec(j) for j in range(1, SECTIONS)]
    barrier = pltpu.get_barrier_semaphore()
    for friend in friends:
        pl.semaphore_signal(barrier, inc=1, device_id=friend, device_id_type=MESH)

    def head_cols(h):
        return pl.ds(h * HD, HD)

    own_copies = [
        pltpu.make_async_copy(stale.at[:, :, head_cols(h)], kv.at[0, h], own_sem.at[h]) for h in range(HEADS)
    ]
    for copy in own_copies:
        copy.start()
    pl.semaphore_wait(barrier, len(friends))
    for copy in own_copies:
        copy.wait()

    def ring(h, d, side, piece):
        rows = pl.ds(piece * ROWS, ROWS)
        into = d if side == 0 else NZ - d
        source = kv.at[0 if d == 1 else d - 1 if side == 0 else NZ - d + 1, h, :, rows, :]
        return pltpu.make_async_remote_copy(
            src_ref=source,
            dst_ref=kv.at[into, h, :, rows, :],
            send_sem=kv_ss.at[side, d, h, piece],
            recv_sem=kv_rs.at[side, d, h, piece],
            device_id=right if side == 0 else left,
            device_id_type=MESH,
        )

    def parts(d):
        return [
            (side, piece) for piece in range(PIECES) for side in range(2)
            if d < HALF or (piece < PIECES // 2) == (side == 0)
        ]

    def arrive(h, d):
        onward = parts(d + 1) if d < HALF else []
        for side, piece in parts(d):
            ring(h, d, side, piece).wait_recv()
            if (side, piece) in onward:
                ring(h, d + 1, side, piece).start()

    for h in range(HEADS):
        for side, piece in parts(1):
            ring(h, 1, side, piece).start()

    def w_send(j):
        to = lax.rem(sec + j, SECTIONS)
        return pltpu.make_async_remote_copy(
            src_ref=w_out.at[:, :, pl.ds(pl.multiple_of(to * COLS, COLS), COLS)],
            dst_ref=w_all.at[:, sec],
            send_sem=w_ss.at[j],
            recv_sem=w_rs.at[j],
            device_id=at_sec(j),
            device_id_type=MESH,
        )

    mod_copy = pltpu.make_async_copy(mod_in, modulation, mod_sem)
    gain_copy = pltpu.make_async_copy(gain_in, gain, gain_sem)
    lat_copy = pltpu.make_async_copy(latent, lat_v, lat_sem)
    for copy in (lat_copy, mod_copy, gain_copy):
        copy.start()
    wq_copies = [pltpu.make_async_copy(w_qkv.at[c], w_v.at[c], wq_sem.at[c]) for c in range(3)]
    for copy in wq_copies:
        copy.start()
    text_copies = [
        pltpu.make_async_copy(text.at[:, :, head_cols(h)], text_v.at[h], text_sem.at[h]) for h in range(HEADS)
    ]
    wo_copy = pltpu.make_async_copy(
        w_out.at[:, :, pl.ds(pl.multiple_of(sec * COLS, COLS), COLS)], w_all.at[:, sec], wo_sem
    )
    for copy in text_copies + [wo_copy]:
        copy.start()

    for j in range(1, SECTIONS):
        w_send(j).start()

    mod_copy.wait()
    def pick_row(rows):
        steps = lax.broadcasted_iota(jnp.int32, rows.shape, 0)
        return jnp.sum(jnp.where(steps == timestep[0], rows.astype(jnp.float32), 0.0), axis=0, keepdims=True)

    shift = pick_row(modulation[:, :WIDTH])
    scale = 1.0 + pick_row(modulation[:, WIDTH : 2 * WIDTH])
    lat_copy.wait()
    gain_copy.wait()

    chunk = 16

    def norm_rows(i, _):
        rows = pl.ds(pl.multiple_of(i * chunk, chunk), chunk)
        x = lat_v[rows, :].astype(jnp.float32)
        centered = x - jnp.mean(x, axis=1, keepdims=True)
        var = jnp.mean(centered * centered, axis=1, keepdims=True)
        normed[rows, :] = (centered * lax.rsqrt(var + 1e-06) * scale + shift).astype(jnp.bfloat16)
        return 0

    lax.fori_loop(0, TOK // chunk, norm_rows, 0)

    def project(c):
        wq_copies[c].wait()
        return jnp.dot(normed[...], w_v[c], preferred_element_type=jnp.float32)

    def head_norm(block, g):
        square = jnp.mean(block * block, axis=-1, keepdims=True)
        return (block * lax.rsqrt(square + 1e-06) * g).astype(jnp.bfloat16)

    def q_send(h, k):
        return pltpu.make_async_remote_copy(
            src_ref=q_all.at[h, 0:TOK, :],
            dst_ref=q_all.at[h, k * TOK : (k + 1) * TOK, :],
            send_sem=q_ss.at[h, k],
            recv_sem=q_rs.at[h, k],
            device_id=at_y(k),
            device_id_type=MESH,
        )

    projected = project(0)
    for h in range(HEADS):
        q_all[h, 0:TOK, :] = head_norm(projected[:, h * HD : (h + 1) * HD], gain[0:1, :])
        for k in range(1, NY):
            q_send(h, k).start()
    arrive(0, 1)
    projected = project(1)
    for h in range(HEADS):
        fresh[h, 0] = head_norm(projected[:, h * HD : (h + 1) * HD], gain[1:2, :])
    arrive(1, 1)
    projected = project(2)
    for h in range(HEADS):
        fresh[h, 1] = projected[:, h * HD : (h + 1) * HD].astype(jnp.bfloat16)
    arrive(2, 1)
    cache_copies = [
        pltpu.make_async_copy(fresh.at[h], next_cache.at[:, :, head_cols(h)], cache_sem.at[h]) for h in range(HEADS)
    ]
    for copy in cache_copies:
        copy.start()

    def attend(h, low, high, blocks, first):
        q = q_all[h, low:high, :]
        logits = []
        for keys, _, live in blocks:
            s = lax.dot_general(keys, q, (((1,), (1,)), ((), ())), preferred_element_type=jnp.float32)
            logits.append(s if live is None else jnp.where(live, s, -jnp.inf))
        best = functools.reduce(jnp.maximum, [jnp.max(s, axis=0, keepdims=True) for s in logits])
        if not first:
            before = top[h, 0:1, low:high]
            best = jnp.maximum(before, best)
        new_acc = new_den = None
        for s, (_, values, _) in zip(logits, blocks):
            p = jnp.exp2((s - best) * SCORE_SCALE)
            part_den = jnp.sum(p, axis=0, keepdims=True)
            part = lax.dot_general(
                values, p.astype(jnp.bfloat16), (((0,), (0,)), ((), ())), preferred_element_type=jnp.float32
            )
            new_acc = part if new_acc is None else new_acc + part
            new_den = part_den if new_den is None else new_den + part_den
        if not first:
            fade = jnp.exp2((before - best) * SCORE_SCALE)
            new_acc = new_acc + acc[h, :, low:high] * fade
            new_den = new_den + den[h, 0:1, low:high] * fade
        acc[h, :, low:high] = new_acc
        den[h, 0:1, low:high] = new_den
        top[h, 0:1, low:high] = best

    def own_step(h):
        for k in range(1, NY):
            q_send(h, k).wait_recv()
        live = lax.broadcasted_iota(jnp.int32, (TXT, TOK), 0) < text_count[0]
        attend(h, 0, TOK, [(fresh[h, 0], fresh[h, 1], None), (text_v[h, 0], text_v[h, 1], live)], True)
        attend(h, TOK, NY * TOK, [(kv[0, h, 0], kv[0, h, 1], None)], True)

    def pair_step(h, d):
        slots = (d, NZ - d) if d < HALF else (d,)
        attend(h, 0, NY * TOK, [(kv[i, h, 0], kv[i, h, 1], None) for i in slots], False)

    def o_copy(h, k, part):
        return pltpu.make_async_remote_copy(
            src_ref=o_send.at[h, k, part],
            dst_ref=o_recv.at[h, k, part],
            send_sem=o_ss.at[h, k, part],
            recv_sem=o_rs.at[h, k, part],
            device_id=at_y(-k),
            device_id_type=MESH,
        )

    def slot_result(h, k, part):
        start = k * TOK + part * PART
        cols = slice(start, start + PART)
        total = den[h, 0:1, cols]
        return acc[h, :, cols] * (1.0 / total), top[h, 0:1, cols] * SCORE_SCALE + jnp.log2(total)

    def rounded(v):
        return v.astype(jnp.bfloat16).astype(jnp.float32)

    def finish(h):
        for part in range(PARTS):
            for k in (2, 1, 3):
                out, lse = slot_result(h, k, part)
                rest = lse - rounded(lse)
                row = lax.broadcasted_iota(jnp.int32, (EXTRA, PART), 0)
                terms = jnp.where(row == 0, lse, jnp.where(row == 1, rest, rest - rounded(rest)))
                o_send[h, k, part, 0:HD, :] = out.astype(jnp.bfloat16)
                o_send[h, k, part, HD:, :] = terms.astype(jnp.bfloat16)
                o_copy(h, k, part).start()

    def a_send(h, j, part):
        return pltpu.make_async_remote_copy(
            src_ref=att.at[h, part, sec],
            dst_ref=att.at[h, part, sec],
            send_sem=a_ss.at[h, j, part],
            recv_sem=a_rs.at[h, j, part],
            device_id=at_sec(j),
            device_id_type=MESH,
        )

    def merge(h, part):
        results = [slot_result(h, 0, part)]
        for k in (1, 3, 2):
            o_copy(h, k, part).wait_recv()
            terms = o_recv[h, k, part, HD:, :].astype(jnp.float32)
            lse = terms[0:1, :] + terms[1:2, :] + terms[2:3, :]
            results.append((o_recv[h, k, part, 0:HD, :].astype(jnp.float32), lse))
        best = functools.reduce(jnp.maximum, [lse for _, lse in results])
        weights = [jnp.exp2(lse - best) for _, lse in results]
        inverse = 1.0 / functools.reduce(jnp.add, weights)
        blend = functools.reduce(jnp.add, [o * (w * inverse) for (o, _), w in zip(results, weights)])
        att[h, part, sec] = blend.astype(jnp.bfloat16)
        for j in (2, 1, 3):
            a_send(h, j, part).start()

    def out_project(h, part):
        for j in (1, 3, 2):
            a_send(h, j, part).wait_recv()
        return lax.dot_general(
            att[h, part].reshape(SECTIONS * HD, PART),
            w_all[h].reshape(SECTIONS * HD, COLS),
            (((0,), (0,)), ((), ())),
            preferred_element_type=jnp.float32,
        )

    for copy in text_copies:
        copy.wait()
    own_step(0)
    own_step(1)
    own_step(2)
    arrive(0, 2)
    pair_step(0, 1)
    arrive(1, 2)
    pair_step(1, 1)
    pair_step(2, 1)
    arrive(0, 3)
    pair_step(0, 2)
    pair_step(0, 3)
    arrive(2, 2)
    pair_step(1, 2)
    arrive(0, 4)
    pair_step(0, 4)
    finish(0)
    arrive(1, 3)
    pair_step(2, 2)
    pair_step(1, 3)
    arrive(2, 3)
    merge(0, 0)
    merge(0, 1)
    pair_step(2, 3)
    arrive(1, 4)
    pair_step(1, 4)
    finish(1)
    arrive(2, 4)
    pair_step(2, 4)
    finish(2)
    merge(1, 0)
    merge(1, 1)
    wo_copy.wait()
    for j in range(1, SECTIONS):
        w_send(j).wait_recv()
    columns = pl.ds(pl.multiple_of(sec * COLS, COLS), COLS)
    gate_row = pick_row(modulation[:, pl.ds(pl.multiple_of(2 * WIDTH + sec * COLS, COLS), COLS)])
    for part in range(PARTS):
        branch[part] = out_project(0, part)
    for part in range(PARTS):
        merge(2, part)
    for part in range(PARTS):
        branch[part] += out_project(1, part)
    for part in range(PARTS):
        rows = slice(part * PART, (part + 1) * PART)
        summed = branch[part] + out_project(2, part)
        layer_out[rows, :] = (lat_v[rows, columns].astype(jnp.float32) + gate_row * summed).astype(jnp.bfloat16)

    for h in range(HEADS):
        for d in range(1, HALF + 1):
            for side, piece in parts(d):
                ring(h, d, side, piece).wait_send()
        for k in range(1, NY):
            q_send(h, k).wait_send()
            for part in range(PARTS):
                o_copy(h, k, part).wait_send()
        for j in range(1, SECTIONS):
            for part in range(PARTS):
                a_send(h, j, part).wait_send()
    for j in range(1, SECTIONS):
        w_send(j).wait_send()
    for copy in cache_copies:
        copy.wait()


def local(latent, stale_kv, text_kv, text_count, timestep, modulation, w_qkv, w_out, norm_gain):
    vmem = pl.BlockSpec(memory_space=pltpu.VMEM)
    smem = pl.BlockSpec(memory_space=pltpu.SMEM)
    hbm = pl.BlockSpec(memory_space=pltpu.HBM)
    bf16, f32 = jnp.bfloat16, jnp.float32
    dma = pltpu.SemaphoreType.DMA
    return pl.pallas_call(
        kernel,
        out_shape=(
            jax.ShapeDtypeStruct((TOK, COLS), bf16),
            jax.ShapeDtypeStruct((2, TOK, HEADS * HD), bf16),
        ),
        in_specs=[smem, smem, hbm, hbm, hbm, hbm, hbm, hbm, hbm],
        out_specs=(vmem, hbm),
        scratch_shapes=[
            pltpu.VMEM((STEPS, 3 * WIDTH), bf16),
            pltpu.VMEM((2, HD), f32),
            pltpu.VMEM((TOK, WIDTH), bf16),
            pltpu.VMEM((TOK, WIDTH), bf16),
            pltpu.VMEM((3, WIDTH, HEADS * HD), bf16),
            pltpu.VMEM((HEADS, 2, TXT, HD), bf16),
            pltpu.VMEM((NZ, HEADS, 2, TOK, HD), bf16),
            pltpu.VMEM((HEADS, 2, TOK, HD), bf16),
            pltpu.VMEM((HEADS, NY * TOK, HD), bf16),
            pltpu.VMEM((HEADS, HD, NY * TOK), f32),
            pltpu.VMEM((HEADS, 8, NY * TOK), f32),
            pltpu.VMEM((HEADS, 8, NY * TOK), f32),
            pltpu.VMEM((HEADS, NY, PARTS, HD + EXTRA, PART), bf16),
            pltpu.VMEM((HEADS, NY, PARTS, HD + EXTRA, PART), bf16),
            pltpu.VMEM((HEADS, PARTS, SECTIONS, HD, PART), bf16),
            pltpu.VMEM((HEADS, SECTIONS, HD, COLS), bf16),
            pltpu.VMEM((PARTS, PART, COLS), f32),
            dma((2, HALF + 1, HEADS, PIECES)), dma((2, HALF + 1, HEADS, PIECES)),
            dma((HEADS, NY)), dma((HEADS, NY)),
            dma((SECTIONS,)), dma((SECTIONS,)),
            dma((HEADS, NY, PARTS)), dma((HEADS, NY, PARTS)),
            dma((HEADS, SECTIONS, PARTS)), dma((HEADS, SECTIONS, PARTS)),
            dma, dma, dma, dma((3,)), dma((HEADS,)), dma((HEADS,)), dma((HEADS,)), dma,
        ],
        compiler_params=pltpu.CompilerParams(
            collective_id=1, has_side_effects=True, vmem_limit_bytes=52 << 20
        ),
    )(
        text_count, timestep, modulation, norm_gain, latent, stale_kv, text_kv,
        w_qkv.transpose(1, 0, 2), w_out.reshape(HEADS, HD, WIDTH),
    )


def solution(mesh):
    in_specs = (
        P(("batch", "blk"), None),
        P(None, ("batch", "blk"), "section"),
        P(None, "batch", "section"),
        P("batch"),
        P("batch"),
        P(),
        P(None, None, "section"),
        P("section", None),
        P(),
    )
    out_specs = (P(("batch", "blk"), "section"), P(None, ("batch", "blk"), "section"))
    return jax.shard_map(local, mesh=mesh, in_specs=in_specs, out_specs=out_specs, check_vma=False)
```

time: 84.8 us -> 63.9 us (0.75)
  Pallas kernels: 78.4 us -> 57.6 us
    pallas_call x1, Pallas kernels: 78.4 us -> 57.6 us  [local(): pl.pallas_call(kernel, out_shape=(jax.ShapeDtypeStruct((TOK, COLS), bf16)...]
where the time goes in v2:
time: 63.9 us; the launch traced here: 63.7 us
  Pallas kernels  57.6 us (90%)
  local copies, waits for them, and re-layouts  4.22 us (7%)
  between operations  1.94 us (3%)
    pallas_call x1, Pallas kernels, local(): pl.pallas_call(kernel, out_shape=(jax.ShapeDtypeStruct((TOK, COLS), bf16)...  57.6 us
    unnamed x8, local copies, waits for them, and re-layouts  4.22 us

profile of v2, /device:TPU:1, one launch (start us, length us, event | category | flops | bytes accessed | tf_op | source)
XLA Modules:
  0.0 63.7 jit_solution(14677177807858920406)
XLA Ops:
  1.9 0.0 copy-start
  1.9 1.1 %copy-done = bf16[28,9216]{1,0:T(8,128)(2,1)S(1)} copy-done((bf16[28,9216]{1,0:T(8,128)(2,1)S(1)}, bf16[28,9216]{1,0:T(8,128)(2,1)}, u32[]{:S(2)}) %copy-start) | copy-done | bytes 516120
  3.0 0.0 copy-start.1
  3.0 1.0 %copy-done.1 = bf16[2,256,384]{2,1,0:T(8,128)(2,1)S(1)} copy-done((bf16[2,256,384]{2,1,0:T(8,128)(2,1)S(1)}, bf16[2,256,384]{2,1,0:T(8,128)(2,1)}, u32[]{:S(2)}) %copy-start.1) | copy-done | bytes 393240
  4.0 0.0 copy-start.2
  4.0 0.7 %copy-done.2 = f32[2,128]{1,0:T(2,128)S(1)} copy-done((f32[2,128]{1,0:T(2,128)S(1)}, f32[2,128]{1,0:T(2,128)}, u32[]{:S(2)}) %copy-start.2) | copy-done | bytes 1048
  4.7 57.6 %shard_map.104 = (bf16[256,768]{1,0:T(8,128)(2,1)S(1)}, bf16[2,256,384]{2,1,0:T(8,128)(2,1)S(1)}) custom-call(s32[1]{0:T(128)S(6)} %copy.13.text_count, s32[1]{0:T(128)S(6)} %copy.14.timestep, bf16[28,9216]{1,0:T(8,128)(2,1)S(1)} %copy-done, f32[2,128]{1,0:T(2,128)S(1)} %copy-done.2, bf16[256,3072]{1,0:T(8,128)(2,1)} %latent.1, ...), custom_call_target="tpu_custom_call" | custom-call | tf_op jit(solution)/shard_map/pallas_call | solution.py:363
  62.2 0.7 %copy.15 = bf16[256,768]{1,0:T(8,128)(2,1)} copy(bf16[256,768]{1,0:T(8,128)(2,1)S(1)} %get-tuple-element.4) | data formatting | bytes 786432
  63.0 0.7 %copy.16 = bf16[2,256,384]{2,1,0:T(8,128)(2,1)} copy(bf16[2,256,384]{2,1,0:T(8,128)(2,1)S(1)} %get-tuple-element.5) | data formatting | bytes 786432
Async XLA Ops:
  1.9 1.1 %copy-start = (bf16[28,9216]{1,0:T(8,128)(2,1)S(1)}, bf16[28,9216]{1,0:T(8,128)(2,1)}, u32[]{:S(2)}) copy-start(bf16[28,9216]{1,0:T(8,128)(2,1)} %mod_in.1) | copy-start | bytes 1548292
  3.0 1.0 %copy-start.1 = (bf16[2,256,384]{2,1,0:T(8,128)(2,1)S(1)}, bf16[2,256,384]{2,1,0:T(8,128)(2,1)}, u32[]{:S(2)}) copy-start(bf16[2,256,384]{2,1,0:T(8,128)(2,1)} %stale.1) | copy-start | bytes 1179652
  4.0 0.7 %copy-start.2 = (f32[2,128]{1,0:T(2,128)S(1)}, f32[2,128]{1,0:T(2,128)}, u32[]{:S(2)}) copy-start(f32[2,128]{1,0:T(2,128)} %gain_in.1) | copy-start | bytes 3076

commit v3 on v2

--- a/solution.py
+++ b/solution.py
@@ -78,10 +78,7 @@
         )
 
     def parts(d):
-        return [
-            (side, piece) for piece in range(PIECES) for side in range(2)
-            if d < HALF or (piece < PIECES // 2) == (side == 0)
-        ]
+        return [(side, side if first else 1 - side) for first in (True, False)[: 2 if d < HALF else 1] for side in range(2)]
 
     def arrive(h, d):
         onward = parts(d + 1) if d < HALF else []
@@ -220,8 +217,7 @@
         attend(h, TOK, NY * TOK, [(kv[0, h, 0], kv[0, h, 1], None)], True)
 
     def pair_step(h, d):
-        slots = (d, NZ - d) if d < HALF else (d,)
-        attend(h, 0, NY * TOK, [(kv[i, h, 0], kv[i, h, 1], None) for i in slots], False)
+        attend(h, 0, NY * TOK, [(kv[i, h, 0], kv[i, h, 1], None) for i in (d, NZ - d)], False)
 
     def o_copy(h, k, part):
         return pltpu.make_async_remote_copy(
@@ -252,6 +248,12 @@
                 o_send[h, k, part, 0:HD, :] = out.astype(jnp.bfloat16)
                 o_send[h, k, part, HD:, :] = terms.astype(jnp.bfloat16)
                 o_copy(h, k, part).start()
+
+    def last_step(h):
+        block = [(kv[HALF, h, 0], kv[HALF, h, 1], None)]
+        attend(h, TOK, NY * TOK, block, False)
+        finish(h)
+        attend(h, 0, TOK, block, False)
 
     def a_send(h, j, part):
         return pltpu.make_async_remote_copy(
@@ -304,8 +306,7 @@
     arrive(2, 2)
     pair_step(1, 2)
     arrive(0, 4)
-    pair_step(0, 4)
-    finish(0)
+    last_step(0)
     arrive(1, 3)
     pair_step(2, 2)
     pair_step(1, 3)
@@ -314,11 +315,9 @@
     merge(0, 1)
     pair_step(2, 3)
     arrive(1, 4)
-    pair_step(1, 4)
-    finish(1)
+    last_step(1)
     arrive(2, 4)
-    pair_step(2, 4)
-    finish(2)
+    last_step(2)
     merge(1, 0)
     merge(1, 1)
     wo_copy.wait()
@@ -394,7 +393,7 @@
             dma, dma, dma, dma((3,)), dma((HEADS,)), dma((HEADS,)), dma((HEADS,)), dma,
         ],
         compiler_params=pltpu.CompilerParams(
-            collective_id=1, has_side_effects=True, vmem_limit_bytes=52 << 20
+            collective_id=1, has_side_effects=True, vmem_limit_bytes=54272 << 10
         ),
     )(
         text_count, timestep, modulation, norm_gain, latent, stale_kv, text_kv,

time: 63.9 us -> 61.9 us (0.969)
  local copies, waits for them, and re-layouts: 4.22 us -> 2.17 us
    unnamed x8 -> x4, local copies, waits for them, and re-layouts: 4.22 us -> 2.17 us
where the time goes in v3:
time: 61.9 us; the launch traced here: 61.8 us
  Pallas kernels  57.7 us (93%)
  local copies, waits for them, and re-layouts  2.17 us (4%)
  between operations  1.94 us (3%)
    pallas_call x1, Pallas kernels, local(): pl.pallas_call(kernel, out_shape=(jax.ShapeDtypeStruct((TOK, COLS), bf16)...  57.7 us
    unnamed x4, local copies, waits for them, and re-layouts  2.17 us

profile of v3, /device:TPU:1, one launch (start us, length us, event | category | flops | bytes accessed | tf_op | source)
XLA Modules:
  0.0 61.8 jit_solution(8108401375974971189)
XLA Ops:
  1.9 0.0 copy-start
  1.9 0.7 %copy-done = f32[2,128]{1,0:T(2,128)S(1)} copy-done((f32[2,128]{1,0:T(2,128)S(1)}, f32[2,128]{1,0:T(2,128)}, u32[]{:S(2)}) %copy-start) | copy-done | bytes 1048
  2.6 57.7 %shard_map.104 = (bf16[256,768]{1,0:T(8,128)(2,1)S(1)}, bf16[2,256,384]{2,1,0:T(8,128)(2,1)S(1)}) custom-call(s32[1]{0:T(128)S(6)} %copy.13.text_count, s32[1]{0:T(128)S(6)} %copy.14.timestep, bf16[28,9216]{1,0:T(8,128)(2,1)} %mod_in.1, f32[2,128]{1,0:T(2,128)S(1)} %copy-done, bf16[256,3072]{1,0:T(8,128)(2,1)} %latent.1, bf16[2,256,384]{2,1,0:T(8,128)(2,1)} %stale.1, ...), custom_call_target="tpu_custom_call" | custom-call | tf_op jit(solution)/shard_map/pallas_call | solution.py:362
  60.3 0.7 %copy.15 = bf16[256,768]{1,0:T(8,128)(2,1)} copy(bf16[256,768]{1,0:T(8,128)(2,1)S(1)} %get-tuple-element.4) | data formatting | bytes 786432
  61.0 0.7 %copy.16 = bf16[2,256,384]{2,1,0:T(8,128)(2,1)} copy(bf16[2,256,384]{2,1,0:T(8,128)(2,1)S(1)} %get-tuple-element.5) | data formatting | bytes 786432
Async XLA Ops:
  1.9 0.7 %copy-start = (f32[2,128]{1,0:T(2,128)S(1)}, f32[2,128]{1,0:T(2,128)}, u32[]{:S(2)}) copy-start(f32[2,128]{1,0:T(2,128)} %gain_in.1) | copy-start | bytes 3076

commit v4 on v3

--- a/solution.py
+++ b/solution.py
@@ -65,7 +65,10 @@
         copy.wait()
 
     def ring(h, d, side, piece):
-        rows = pl.ds(piece * ROWS, ROWS)
+        if piece < PIECES:
+            rows = pl.ds(piece * ROWS, ROWS)
+        else:
+            rows = pl.ds(side * ROWS + (piece - PIECES) * (ROWS // 2), ROWS // 2)
         into = d if side == 0 else NZ - d
         source = kv.at[0 if d == 1 else d - 1 if side == 0 else NZ - d + 1, h, :, rows, :]
         return pltpu.make_async_remote_copy(
@@ -77,18 +80,23 @@
             device_id_type=MESH,
         )
 
-    def parts(d):
-        return [(side, side if first else 1 - side) for first in (True, False)[: 2 if d < HALF else 1] for side in range(2)]
+    def parts(h, d):
+        quarters = h == HEADS - 1 and d >= HALF - 1
+        onward = [(s, p) for p in (2, 3) for s in range(2)] if quarters else [(s, s) for s in range(2)]
+        return onward + ([(s, 1 - s) for s in range(2)] if d < HALF else [])
 
     def arrive(h, d):
-        onward = parts(d + 1) if d < HALF else []
-        for side, piece in parts(d):
+        onward = parts(h, d + 1) if d < HALF else []
+        for side, piece in parts(h, d):
             ring(h, d, side, piece).wait_recv()
             if (side, piece) in onward:
                 ring(h, d + 1, side, piece).start()
+            elif piece == side and (side, 2) in onward:
+                ring(h, d + 1, side, 2).start()
+                ring(h, d + 1, side, 3).start()
 
     for h in range(HEADS):
-        for side, piece in parts(1):
+        for side, piece in parts(h, 1):
             ring(h, 1, side, piece).start()
 
     def w_send(j):
@@ -303,19 +311,19 @@
     arrive(0, 3)
     pair_step(0, 2)
     pair_step(0, 3)
-    arrive(2, 2)
+    arrive(1, 3)
     pair_step(1, 2)
     arrive(0, 4)
     last_step(0)
-    arrive(1, 3)
+    arrive(2, 2)
+    pair_step(1, 3)
+    arrive(1, 4)
+    last_step(1)
     pair_step(2, 2)
-    pair_step(1, 3)
     arrive(2, 3)
     merge(0, 0)
     merge(0, 1)
     pair_step(2, 3)
-    arrive(1, 4)
-    last_step(1)
     arrive(2, 4)
     last_step(2)
     merge(1, 0)
@@ -338,7 +346,7 @@
 
     for h in range(HEADS):
         for d in range(1, HALF + 1):
-            for side, piece in parts(d):
+            for side, piece in parts(h, d):
                 ring(h, d, side, piece).wait_send()
         for k in range(1, NY):
             q_send(h, k).wait_send()
@@ -385,7 +393,7 @@
             pltpu.VMEM((HEADS, PARTS, SECTIONS, HD, PART), bf16),
             pltpu.VMEM((HEADS, SECTIONS, HD, COLS), bf16),
             pltpu.VMEM((PARTS, PART, COLS), f32),
-            dma((2, HALF + 1, HEADS, PIECES)), dma((2, HALF + 1, HEADS, PIECES)),
+            dma((2, HALF + 1, HEADS, 4)), dma((2, HALF + 1, HEADS, 4)),
             dma((HEADS, NY)), dma((HEADS, NY)),
             dma((SECTIONS,)), dma((SECTIONS,)),
             dma((HEADS, NY, PARTS)), dma((HEADS, NY, PARTS)),

time: 61.9 us -> 63.6 us (1.027)
  Pallas kernels: 57.7 us -> 59.4 us
    pallas_call x1, Pallas kernels: 57.7 us -> 59.4 us  [local(): pl.pallas_call(kernel, out_shape=(jax.ShapeDtypeStruct((TOK, COLS), bf16)...]
where the time goes in v4:
time: 63.6 us; the launch traced here: 63.5 us
  Pallas kernels  59.4 us (93%)
  local copies, waits for them, and re-layouts  2.17 us (3%)
  between operations  1.94 us (3%)
    pallas_call x1, Pallas kernels, local(): pl.pallas_call(kernel, out_shape=(jax.ShapeDtypeStruct((TOK, COLS), bf16)...  59.4 us
    unnamed x4, local copies, waits for them, and re-layouts  2.17 us

profile of v4, /device:TPU:1, one launch (start us, length us, event | category | flops | bytes accessed | tf_op | source)
XLA Modules:
  0.0 63.5 jit_solution(5099418468443136739)
XLA Ops:
  1.9 0.0 copy-start
  1.9 0.7 %copy-done = f32[2,128]{1,0:T(2,128)S(1)} copy-done((f32[2,128]{1,0:T(2,128)S(1)}, f32[2,128]{1,0:T(2,128)}, u32[]{:S(2)}) %copy-start) | copy-done | bytes 1048
  2.6 59.4 %shard_map.104 = (bf16[256,768]{1,0:T(8,128)(2,1)S(1)}, bf16[2,256,384]{2,1,0:T(8,128)(2,1)S(1)}) custom-call(s32[1]{0:T(128)S(6)} %copy.13.text_count, s32[1]{0:T(128)S(6)} %copy.14.timestep, bf16[28,9216]{1,0:T(8,128)(2,1)} %mod_in.1, f32[2,128]{1,0:T(2,128)S(1)} %copy-done, bf16[256,3072]{1,0:T(8,128)(2,1)} %latent.1, bf16[2,256,384]{2,1,0:T(8,128)(2,1)} %stale.1, ...), custom_call_target="tpu_custom_call" | custom-call | tf_op jit(solution)/shard_map/pallas_call | solution.py:370
  62.0 0.7 %copy.15 = bf16[256,768]{1,0:T(8,128)(2,1)} copy(bf16[256,768]{1,0:T(8,128)(2,1)S(1)} %get-tuple-element.4) | data formatting | bytes 786432
  62.7 0.7 %copy.16 = bf16[2,256,384]{2,1,0:T(8,128)(2,1)} copy(bf16[2,256,384]{2,1,0:T(8,128)(2,1)S(1)} %get-tuple-element.5) | data formatting | bytes 786432
Async XLA Ops:
  1.9 0.7 %copy-start = (f32[2,128]{1,0:T(2,128)S(1)}, f32[2,128]{1,0:T(2,128)}, u32[]{:S(2)}) copy-start(f32[2,128]{1,0:T(2,128)} %gain_in.1) | copy-start | bytes 3076
